TPU v7x, 32 devices: a whole 2x2x4 slice. The times are simulated.
32 devices in a mesh: wl: 4 (over y, x), tile: 8 (over z, core).
Axes of the slice: x: 2, y: 2, z: 4, core: 2. Of those that a mesh axis runs over, the one named last changes fastest.
Arguments:
- density: float32 [16, 1024], P('tile', 'wl'), may hold values from 0 to 1
- foot_index: int32 [4, 64, 4096], P(None, 'tile'), may hold values from 0 to 2047, as said below
- foot_weight: bfloat16 [4, 64, 4096], P(None, 'tile'), may hold values from 0.099609375 to 0.3984375
- source_fwd: float32 [8, 64, 4096], P('wl', 'tile'), may hold values from -6 to 6
- source_adj: float32 [8, 64, 4096], P('wl', 'tile'), may hold values from -6 to 6
- omega: float32 [8], P('wl'), may hold values from 0.2 to 1.5
Outputs:
- forward_field: float32 [8, 64, 4096], P('wl', 'tile')
- density_grad: float32 [16, 1024], P('tile', 'wl')
Inputs may be any that keep to these rules, and one draw needn't show every extreme that they name: foot_index[f, x, y] = r * 1024 + c names coarse row r and column c of the strip of the tile holding row x, with r within one of (x mod 8) // 4 and c within two of y // 4; entry f = 0 is the cell's own block.
All inputs are finite; a program needn't handle non-finite values.
Results may differ from a plain program's by a relative error of at most 0.0003.
Values sent between devices are 32-bit elements; how exact they have to be, the bound alone decides.
A program may use at most 192 MiB of HBM per device.

v0:
```python
import functools

import jax
import jax.numpy as jnp
from jax import lax
from jax.experimental import pallas as pl
from jax.experimental.pallas import tpu as pltpu
from jax.sharding import PartitionSpec as P

ITERS = 4
CELLS = 4
REACH = 2
OFFSETS = 2 * REACH + 1
LANES = 128
WIDTH = CELLS * LANES

time_step = 0.5
high_contrast = 4.0
drude_decay = 0.9
drude_gain = 0.5

MESH = pl.DeviceIdType.MESH


def kernel(
    n_wl, n_tile, n_wave, cols, blocks, strip,
    dens_hbm, index_hbm, weight_hbm, fwd_hbm, adj_hbm, omega,
    field_hbm, grad_out,
    gathered, index, weight, src, table, density, inverse, matched, pool, drive,
    edge_src, field1, field2, field3, edge, curl, current, final, pooled,
    send_near, send_far, recv_near, recv_far, send_dens, recv_dens,
    part, part_in,
    local_sem, gather_send, gather_recv, halo_send, halo_recv, part_send, part_recv,
):
    wl = lax.axis_index("wl")
    tile = lax.axis_index("tile")
    piece = blocks // n_wl
    chunks = cols // WIDTH
    has_above, has_below = tile > 0, tile < n_tile - 1

    loads = [
        pltpu.make_async_copy(fwd_hbm, src.at[0], local_sem.at[0]),
        pltpu.make_async_copy(adj_hbm, src.at[1], local_sem.at[1]),
        pltpu.make_async_copy(dens_hbm, gathered.at[wl], local_sem.at[2]),
        pltpu.make_async_copy(index_hbm, index, local_sem.at[3]),
        pltpu.make_async_copy(weight_hbm, weight, local_sem.at[4]),
    ]
    for load in loads:
        load.start()

    barrier = pltpu.get_barrier_semaphore()
    peers = [lax.rem(wl + k, n_wl) for k in range(1, n_wl)]
    for peer in peers:
        pl.semaphore_signal(barrier, inc=1, device_id={"wl": peer}, device_id_type=MESH)

    @pl.when(has_above)
    def _():
        pl.semaphore_signal(barrier, inc=1, device_id={"tile": tile - 1}, device_id_type=MESH)

    @pl.when(has_below)
    def _():
        pl.semaphore_signal(barrier, inc=1, device_id={"tile": tile + 1}, device_id_type=MESH)

    loads[0].wait()
    loads[1].wait()
    for w in range(n_wave):
        for run in range(2):
            k = 2 * w + run
            send_near[0, 2 * k : 2 * k + 2, :] = src[run, w, 0:2, :]
            send_far[0, k : k + 1, :] = src[run, w, 2:3, :]
            send_near[1, 2 * k : 2 * k + 2, :] = src[run, w, 6:8, :]
            send_far[1, k : k + 1, :] = src[run, w, 5:6, :]

    @pl.when(tile == 0)
    def _():
        recv_near[1] = jnp.zeros_like(recv_near[1])
        recv_far[1] = jnp.zeros_like(recv_far[1])
        recv_dens[1] = jnp.zeros_like(recv_dens[1])

    @pl.when(tile == n_tile - 1)
    def _():
        recv_near[0] = jnp.zeros_like(recv_near[0])
        recv_far[0] = jnp.zeros_like(recv_far[0])
        recv_dens[0] = jnp.zeros_like(recv_dens[0])

    @pl.when(has_above & has_below)
    def _():
        pl.semaphore_wait(barrier, n_wl + 1)

    @pl.when(jnp.logical_not(has_above & has_below))
    def _():
        pl.semaphore_wait(barrier, n_wl)

    def gather_to(peer, slot):
        return pltpu.make_async_remote_copy(
            src_ref=dens_hbm, dst_ref=gathered.at[slot],
            send_sem=gather_send.at[peer], recv_sem=gather_recv.at[slot],
            device_id={"wl": peer}, device_id_type=MESH,
        )

    for peer in peers:
        gather_to(peer, wl).start()

    def halo(way, kind, source, target):
        other = tile - 1 if way == 0 else tile + 1
        return pltpu.make_async_remote_copy(
            src_ref=source.at[way], dst_ref=target.at[way],
            send_sem=halo_send.at[way, kind], recv_sem=halo_recv.at[way, kind],
            device_id={"tile": other}, device_id_type=MESH,
        )

    copies = ((send_near, recv_near), (send_far, recv_far), (send_dens, recv_dens))

    def sends(kinds, act):
        for way, there in ((0, has_above), (1, has_below)):
            @pl.when(there)
            def _():
                for kind in kinds:
                    act(halo(way, kind, *copies[kind]))

    def arrivals(kinds):
        for way, there in ((0, has_below), (1, has_above)):
            @pl.when(there)
            def _():
                for kind in kinds:
                    halo(way, kind, *copies[kind]).wait_recv()

    sends((0, 1), lambda copy: copy.start())

    row = lax.broadcasted_iota(jnp.int32, (8, LANES), 0)
    lane = lax.broadcasted_iota(jnp.int32, (8, LANES), 1)
    arg = jnp.zeros((8, LANES), jnp.float32)
    for w in range(n_wave):
        turn = (row - w * ITERS + 1).astype(jnp.float32)
        inside = (row >= w * ITERS) & (row < (w + 1) * ITERS)
        arg = jnp.where(inside, omega[w] * turn, arg)
    waves = jnp.sin(arg)
    for w in range(n_wave):
        for t in range(ITERS):
            k = w * ITERS + t
            drive[k] = jnp.broadcast_to(waves[k : k + 1, :], (8, LANES))
    cell = lax.broadcasted_iota(jnp.int32, (WIDTH, LANES), 0) // CELLS
    block = lax.broadcasted_iota(jnp.int32, (WIDTH, LANES), 1)
    pool[...] = (cell == block).astype(jnp.float32).astype(jnp.bfloat16)
    for field in (field1, field2, field3):
        for w in range(n_wave):
            for s in range(3):
                field[w, s, :, LANES + cols :] = jnp.zeros((8, LANES), jnp.float32)
    table[:, :, :LANES] = jnp.zeros((2, 8, LANES), jnp.float32)
    table[:, :, LANES + blocks :] = jnp.zeros((2, 8, LANES), jnp.float32)

    def spread(w, t):
        return jnp.concatenate([drive[w * ITERS + t]] * CELLS, axis=1)

    loads[2].wait()
    loads[3].wait()
    loads[4].wait()
    for peer in peers:
        gather_to(wl, peer).wait_recv()
    for i in range(n_wl):
        for r in range(2):
            table[r, :, LANES + piece * i : LANES + piece * (i + 1)] = jnp.broadcast_to(
                gathered[i, r : r + 1, :], (8, piece)
            )

    low = lane < LANES // 2
    keep_early = (lane >= 16) & (lane < 80)
    keep_late = (lane >= 48) & (lane < 112)

    def half(x):
        return pltpu.roll(x, LANES // 2, 1)

    def cell_density(g, carry):
        at = pl.multiple_of(g * LANES, LANES)
        before = [table[r, :, pl.ds(at, LANES)] for r in range(2)]
        here = [table[r, :, pl.ds(at + LANES, LANES)] for r in range(2)]
        after = [table[r, :, pl.ds(at + 2 * LANES, LANES)] for r in range(2)]
        turned = [half(before[0]), half(here[0]), half(after[0])]
        turned_row = half(here[1])
        tables = [
            jnp.where(keep_late, jnp.where(low, turned[0], turned[1]), jnp.where(low, here[1], before[1])),
            jnp.where(keep_early, here[0], turned_row),
            jnp.where(keep_late, here[0], turned_row),
            jnp.where(keep_early, jnp.where(low, turned[1], turned[2]), jnp.where(low, after[1], here[1])),
        ]
        for q in range(CELLS):
            start = pl.multiple_of(g * WIDTH + q * LANES, LANES)
            total = jnp.zeros((8, LANES), jnp.float32)
            for f in range(index.shape[0]):
                entry = index[f, :, pl.ds(start, LANES)]
                below = jnp.where(entry >= blocks, LANES // 2, 0)
                place = (entry + below + (LANES // 2 if q in (0, 3) else 0)) & (LANES - 1)
                value = jnp.take_along_axis(tables[q], place, axis=1, mode="promise_in_bounds")
                total = total + weight[f, :, pl.ds(start, LANES)].astype(jnp.float32) * value
            density[0, :, pl.ds(start, LANES)] = total
            inverse[0, :, pl.ds(start, LANES)] = time_step / (1.0 + high_contrast * total)
        return carry

    lax.fori_loop(0, chunks, cell_density, 0)
    send_dens[0] = density[0, 0:2, :]
    send_dens[1] = density[0, 6:8, :]
    sends((2,), lambda copy: copy.start())

    own = lax.broadcasted_iota(jnp.int32, (8, LANES), 1) // CELLS

    def weigh(g, carry):
        start = pl.multiple_of(g * LANES, LANES)
        base = own + g * (LANES // CELLS)
        shifts = [index[f, :, pl.ds(start, LANES)] - base for f in range(index.shape[0])]
        values = [weight[f, :, pl.ds(start, LANES)].astype(jnp.float32) for f in range(index.shape[0])]
        for r in range(2):
            for d in range(OFFSETS):
                target = r * blocks + d - REACH
                total = jnp.where(shifts[0] == target, values[0], 0.0)
                for f in range(1, index.shape[0]):
                    total = total + jnp.where(shifts[f] == target, values[f], 0.0)
                matched[r * OFFSETS + d, :, pl.ds(start, LANES)] = total
        return carry

    lax.fori_loop(0, cols // LANES, weigh, 0)

    arrivals((0, 1))
    for w in range(n_wave):
        for run in range(2):
            k = 2 * w + run
            edge_src[w, 2, 4 * run : 4 * run + 2, :] = recv_near[1, 2 * k : 2 * k + 2, :]
            edge_src[w, 2, 4 * run + 2 : 4 * run + 4, :] = recv_near[0, 2 * k : 2 * k + 2, :]
            edge[w, 2, 4 * run : 4 * run + 1, :] = recv_far[1, k : k + 1, :]
            edge[w, 2, 4 * run + 1 : 4 * run + 2, :] = src[run, w, 0:1, :]
            edge[w, 2, 4 * run + 2 : 4 * run + 3, :] = src[run, w, 7:8, :]
            edge[w, 2, 4 * run + 3 : 4 * run + 4, :] = recv_far[0, k : k + 1, :]

    first = tile == 0

    def rim(w, own_rows, halo_rows, where):
        for run in range(2):
            e = own_rows[run]
            above = jnp.where(first, e[0:1, :], halo_rows[4 * run + 1 : 4 * run + 2, :])
            edge[w, run, 0:1, where] = above
            edge[w, run, 7:8, where] = halo_rows[4 * run + 2 : 4 * run + 3, :]

    def start_fields(g, carry):
        where = pl.ds(pl.multiple_of(g * WIDTH, WIDTH), WIDTH)
        inner = pl.ds(pl.multiple_of(g * WIDTH + LANES, LANES), WIDTH)
        for w in range(n_wave):
            level = spread(w, 0)
            slabs = [level * src[0, w, :, where], level * src[1, w, :, where], level * edge_src[w, 2, :, where]]
            for s in range(3):
                field1[w, s, :, inner] = slabs[s]
            edge[w, 2, :, where] = level * edge[w, 2, :, where]
            rim(w, slabs, slabs[2], where)
        return carry

    lax.fori_loop(0, chunks, start_fields, 0)

    def mirror(field):
        for w in range(n_wave):
            for s in range(3):
                field[w, s, :, 0:LANES] = jnp.broadcast_to(field[w, s, :, LANES : LANES + 1], (8, LANES))

    mirror(field1)

    arrivals((2,))
    for k in range(2):
        density[1, 4 * k : 4 * k + 2, :] = recv_dens[1]
        density[1, 4 * k + 2 : 4 * k + 4, :] = recv_dens[0]

    wide_row = lax.broadcasted_iota(jnp.int32, (8, WIDTH), 0)
    beyond = (tile == n_tile - 1) & ((wide_row & 3) >= 2)
    odd = (wide_row & 1) == 1
    top = wide_row == 0
    bottom = wide_row == 7

    def invert(g, carry):
        where = pl.ds(pl.multiple_of(g * WIDTH, WIDTH), WIDTH)
        inverse[1, :, where] = jnp.where(beyond, 0.0, time_step / (1.0 + high_contrast * density[1, :, where]))
        return carry

    lax.fori_loop(0, chunks, invert, 0)

    def advance(t, old, g, w, s):
        where = pl.ds(pl.multiple_of(g * WIDTH, WIDTH), WIDTH)
        window = old[w, s, :, pl.ds(pl.multiple_of(g * WIDTH, WIDTH), WIDTH + 2 * LANES)]
        e = window[:, LANES : LANES + WIDTH]
        left = pltpu.roll(window, 1, 1)[:, LANES : LANES + WIDTH]
        right = pltpu.roll(window, WIDTH + 2 * LANES - 1, 1)[:, LANES : LANES + WIDTH]
        rows = edge[w, s, :, where]
        up = jnp.where(odd if s == 2 else bottom, rows, pltpu.roll(e, 7, 0))
        down = jnp.where((~odd) if s == 2 else top, rows, pltpu.roll(e, 1, 0))
        half_of = 1 if s == 2 else 0
        dens = density[half_of, :, where]
        c = time_step * (((up + down) + (left + right)) - 4.0 * e)
        j = (drude_gain * dens) * e
        if t > 1:
            c = c + curl[w, s, :, where]
            j = j + drude_decay * current[w, s, :, where]
        if t < ITERS - 1:
            curl[w, s, :, where] = c
            current[w, s, :, where] = j
        source = edge_src[w, 2, :, where] if s == 2 else src[s, w, :, where]
        return e + inverse[half_of, :, where] * (c - j) + spread(w, t) * source

    for t, old, new in ((1, field1, field2), (2, field2, field3)):
        def step(g, carry, t=t, old=old, new=new):
            where = pl.ds(pl.multiple_of(g * WIDTH, WIDTH), WIDTH)
            inner = pl.ds(pl.multiple_of(g * WIDTH + LANES, LANES), WIDTH)
            for w in range(n_wave):
                slabs = [advance(t, old, g, w, s) for s in range(3)]
                for s in range(3):
                    new[w, s, :, inner] = slabs[s]
                rim(w, slabs, slabs[2], where)
                for run in range(2):
                    edge[w, 2, 4 * run + 1 : 4 * run + 2, where] = slabs[run][0:1, :]
                    edge[w, 2, 4 * run + 2 : 4 * run + 3, where] = slabs[run][7:8, :]
            return carry

        lax.fori_loop(0, chunks, step, 0)
        mirror(new)

    def last(g, carry):
        where = pl.ds(pl.multiple_of(g * WIDTH, WIDTH), WIDTH)
        inner = pl.ds(pl.multiple_of(g * WIDTH + LANES, LANES), WIDTH)
        sense = jnp.zeros((8, WIDTH), jnp.float32)
        for w in range(n_wave):
            end_fwd = advance(ITERS - 1, field3, g, w, 0)
            end_adj = advance(ITERS - 1, field3, g, w, 1)
            final[w, :, where] = end_fwd
            sense = sense + (
                field1[w, 1, :, inner] * end_fwd
                + field2[w, 1, :, inner] * field3[w, 0, :, inner]
                + field3[w, 1, :, inner] * field2[w, 0, :, inner]
                + end_adj * field1[w, 0, :, inner]
            )
        terms = jnp.concatenate([matched[k, :, where] * sense for k in range(2 * OFFSETS)], axis=0)
        coarse = terms.astype(jnp.bfloat16)
        fine = (terms - coarse.astype(jnp.float32)).astype(jnp.bfloat16)
        sums = jnp.dot(coarse, pool[...], preferred_element_type=jnp.float32) + jnp.dot(
            fine, pool[...], preferred_element_type=jnp.float32
        )
        out = pl.ds(pl.multiple_of(g * LANES, LANES), LANES)
        for k in range(2 * OFFSETS):
            pooled[k, :, out] = sums[8 * k : 8 * k + 8, :]
        return carry

    lax.fori_loop(0, chunks, last, 0)
    store = pltpu.make_async_copy(final, field_hbm, local_sem.at[5])
    store.start()

    for r in range(2):
        total = pooled[r * OFFSETS + REACH]
        for d in range(-REACH, REACH + 1):
            if d:
                total = total + pltpu.roll(pooled[r * OFFSETS + REACH + d], d % blocks, 1)
        line = (high_contrast / (n_wl * n_wave)) * jnp.sum(total, axis=0, keepdims=True)
        for i in range(n_wl):
            part[i, r : r + 1, :] = line[:, piece * i : piece * (i + 1)]

    def part_to(peer, slot):
        return pltpu.make_async_remote_copy(
            src_ref=part.at[peer], dst_ref=part_in.at[slot],
            send_sem=part_send.at[peer], recv_sem=part_recv.at[slot],
            device_id={"wl": peer}, device_id_type=MESH,
        )

    for peer in peers:
        part_to(peer, wl).start()
    part_in[wl] = part[wl]
    for peer in peers:
        part_to(wl, peer).wait_recv()
    total = part_in[0]
    for i in range(1, n_wl):
        total = total + part_in[i]
    grad_out[...] = total

    for peer in peers:
        gather_to(peer, wl).wait_send()
        part_to(peer, wl).wait_send()
    sends((0, 1, 2), lambda copy: copy.wait_send())
    store.wait()


def shards(n_wl, n_tile, density, foot_index, foot_weight, source_fwd, source_adj, omega):
    n_wave, rows, cols = source_fwd.shape
    feet = foot_index.shape[0]
    strip, piece = density.shape
    blocks = piece * n_wl
    f32 = jnp.float32
    anywhere = pl.BlockSpec(memory_space=pl.ANY)
    padded = cols + 2 * LANES
    vmem = pltpu.VMEM
    dma = pltpu.SemaphoreType.DMA
    return pl.pallas_call(
        functools.partial(kernel, n_wl, n_tile, n_wave, cols, blocks, strip),
        out_shape=(
            jax.ShapeDtypeStruct(source_fwd.shape, f32),
            jax.ShapeDtypeStruct(density.shape, f32),
        ),
        in_specs=[anywhere] * 5 + [pl.BlockSpec(memory_space=pltpu.SMEM)],
        out_specs=(anywhere, pl.BlockSpec(memory_space=pltpu.VMEM)),
        scratch_shapes=[
            vmem((n_wl, strip, piece), f32),
            vmem((feet, rows, cols), jnp.int32),
            vmem((feet, rows, cols), jnp.bfloat16),
            vmem((2, n_wave, rows, cols), f32),
            vmem((2, 8, blocks + 2 * LANES), f32),
            vmem((2, rows, cols), f32),
            vmem((2, rows, cols), f32),
            vmem((2 * OFFSETS, rows, cols), f32),
            vmem((WIDTH, LANES), jnp.bfloat16),
            vmem((n_wave * ITERS, 8, LANES), f32),
            vmem((n_wave, 3, rows, cols), f32),
            vmem((n_wave, 3, rows, padded), f32),
            vmem((n_wave, 3, rows, padded), f32),
            vmem((n_wave, 3, rows, padded), f32),
            vmem((n_wave, 3, rows, cols), f32),
            vmem((n_wave, 3, rows, cols), f32),
            vmem((n_wave, 3, rows, cols), f32),
            vmem((n_wave, rows, cols), f32),
            vmem((2 * OFFSETS, rows, blocks), f32),
            vmem((2, 4 * n_wave, cols), f32),
            vmem((2, 2 * n_wave, cols), f32),
            vmem((2, 4 * n_wave, cols), f32),
            vmem((2, 2 * n_wave, cols), f32),
            vmem((2, 2, cols), f32),
            vmem((2, 2, cols), f32),
            vmem((n_wl, strip, piece), f32),
            vmem((n_wl, strip, piece), f32),
            dma((6,)),
            dma((n_wl,)),
            dma((n_wl,)),
            dma((2, 3)),
            dma((2, 3)),
            dma((n_wl,)),
            dma((n_wl,)),
        ],
        compiler_params=pltpu.CompilerParams(
            collective_id=0, has_side_effects=True, vmem_limit_bytes=48 * 1024 * 1024
        ),
        cost_estimate=pl.CostEstimate(flops=40_000_000, bytes_accessed=2_000_000, transcendentals=0),
    )(density, foot_index, foot_weight, source_fwd, source_adj, omega)


def solution(mesh):
    in_specs = (
        P("tile", "wl"),
        P(None, "tile", None),
        P(None, "tile", None),
        P("wl", "tile", None),
        P("wl", "tile", None),
        P("wl"),
    )
    out_specs = (P("wl", "tile", None), P("tile", "wl"))
    body = functools.partial(shards, mesh.shape["wl"], mesh.shape["tile"])
    return jax.shard_map(body, mesh=mesh, in_specs=in_specs, out_specs=out_specs, check_vma=False)
```

profile of v0, /device:TPU:1, one launch (start us, length us, event | category | flops | bytes accessed | tf_op | source)
XLA Modules:
  0.0 27.0 jit_solution(18343027510913760382)
XLA Ops:
  0.6 0.0 copy-start
  0.6 1.0 %copy-done = s32[4,8,4096]{2,1,0:T(8,128)S(1)} copy-done((s32[4,8,4096]{2,1,0:T(8,128)S(1)}, s32[4,8,4096]{2,1,0:T(8,128)}, u32[]{:S(2)}) %copy-start) | copy-done | bytes 524312
  1.7 0.0 copy-start.1
  1.7 0.9 %copy-done.1 = bf16[4,8,4096]{2,1,0:T(8,128)(2,1)S(1)} copy-done((bf16[4,8,4096]{2,1,0:T(8,128)(2,1)S(1)}, bf16[4,8,4096]{2,1,0:T(8,128)(2,1)}, u32[]{:S(2)}) %copy-start.1) | copy-done | bytes 262168
  2.6 0.0 copy-start.2
  2.6 0.9 %copy-done.2 = f32[2,8,4096]{2,1,0:T(8,128)S(1)} copy-done((f32[2,8,4096]{2,1,0:T(8,128)S(1)}, f32[2,8,4096]{2,1,0:T(8,128)}, u32[]{:S(2)}) %copy-start.2) | copy-done | bytes 262168
  3.6 0.0 copy-start.3
  3.6 0.9 %copy-done.3 = f32[2,8,4096]{2,1,0:T(8,128)S(1)} copy-done((f32[2,8,4096]{2,1,0:T(8,128)S(1)}, f32[2,8,4096]{2,1,0:T(8,128)}, u32[]{:S(2)}) %copy-start.3) | copy-done | bytes 262168
  4.5 0.0 copy-start.4
  4.5 0.7 %copy-done.4 = f32[2,256]{1,0:T(2,128)S(1)} copy-done((f32[2,256]{1,0:T(2,128)S(1)}, f32[2,256]{1,0:T(2,128)}, u32[]{:S(2)}) %copy-start.4) | copy-done | bytes 2072
  5.2 0.0 copy-start.5
  5.2 0.7 %copy-done.5 = f32[2]{0:T(128)S(1)} copy-done((f32[2]{0:T(128)S(1)}, f32[2]{0:T(128)}, u32[]{:S(2)}) %copy-start.5) | copy-done | bytes 32
  5.9 19.8 %shard_map.77 = (f32[2,8,4096]{2,1,0:T(8,128)S(1)}, f32[2,256]{1,0:T(2,128)S(1)}) custom-call(f32[2,256]{1,0:T(2,128)S(1)} %copy-done.4, s32[4,8,4096]{2,1,0:T(8,128)S(1)} %copy-done, bf16[4,8,4096]{2,1,0:T(8,128)(2,1)S(1)} %copy-done.1, f32[2,8,4096]{2,1,0:T(8,128)S(1)} %copy-done.2, f32[2,8,4096]{2,1,0:T(8,128)S(1)} %copy-done.3, f32[2]{0:T(128)S(1)} %copy-done.5), custom_call_target="tpu_custom_call" | custom-call | flops 40000000 | bytes 2000000 | tf_op jit(solution)/shard_map/pallas_call | solution.py:392
  25.7 0.7 %copy.10 = f32[2,8,4096]{2,1,0:T(8,128)} copy(f32[2,8,4096]{2,1,0:T(8,128)S(1)} %get-tuple-element.4) | data formatting | bytes 524288
  26.4 0.6 %copy.11 = f32[2,256]{1,0:T(2,128)} copy(f32[2,256]{1,0:T(2,128)S(1)} %get-tuple-element.5) | data formatting | bytes 4096
Async XLA Ops:
  0.6 1.0 %copy-start = (s32[4,8,4096]{2,1,0:T(8,128)S(1)}, s32[4,8,4096]{2,1,0:T(8,128)}, u32[]{:S(2)}) copy-start(s32[4,8,4096]{2,1,0:T(8,128)} %index_hbm.1) | copy-start | bytes 1572868
  1.7 0.9 %copy-start.1 = (bf16[4,8,4096]{2,1,0:T(8,128)(2,1)S(1)}, bf16[4,8,4096]{2,1,0:T(8,128)(2,1)}, u32[]{:S(2)}) copy-start(bf16[4,8,4096]{2,1,0:T(8,128)(2,1)} %weight_hbm.1) | copy-start | bytes 786436
  2.6 0.9 %copy-start.2 = (f32[2,8,4096]{2,1,0:T(8,128)S(1)}, f32[2,8,4096]{2,1,0:T(8,128)}, u32[]{:S(2)}) copy-start(f32[2,8,4096]{2,1,0:T(8,128)} %fwd_hbm.1) | copy-start | bytes 786436
  3.6 0.9 %copy-start.3 = (f32[2,8,4096]{2,1,0:T(8,128)S(1)}, f32[2,8,4096]{2,1,0:T(8,128)}, u32[]{:S(2)}) copy-start(f32[2,8,4096]{2,1,0:T(8,128)} %adj_hbm.1) | copy-start | bytes 786436
  4.5 0.7 %copy-start.4 = (f32[2,256]{1,0:T(2,128)S(1)}, f32[2,256]{1,0:T(2,128)}, u32[]{:S(2)}) copy-start(f32[2,256]{1,0:T(2,128)} %dens_hbm.1) | copy-start | bytes 6148
  5.2 0.7 %copy-start.5 = (f32[2]{0:T(128)S(1)}, f32[2]{0:T(128)}, u32[]{:S(2)}) copy-start(f32[2]{0:T(128)} %omega.1) | copy-start | bytes 28
where the time goes:
time: 27.3 us; the launch traced here: 27 us
  Pallas kernels  19.8 us (73%)
  local copies, waits for them, and re-layouts  6.5 us (24%)
  between operations  0.65 us (2%)
    pallas_call x1, Pallas kernels, shards(): pl.pallas_call(functools.partial(kernel, n_wl, n_tile, n_wave, cols, bloc...  19.8 us
    unnamed x14, local copies, waits for them, and re-layouts  6.5 us

commit v1 on v0

--- a/solution.py
+++ b/solution.py
@@ -434,7 +434,7 @@
             dma((n_wl,)),
         ],
         compiler_params=pltpu.CompilerParams(
-            collective_id=0, has_side_effects=True, vmem_limit_bytes=48 * 1024 * 1024
+            collective_id=0, has_side_effects=True
         ),
         cost_estimate=pl.CostEstimate(flops=40_000_000, bytes_accessed=2_000_000, transcendentals=0),
     )(density, foot_index, foot_weight, source_fwd, source_adj, omega)

time: 27.3 us -> 23.9 us (0.88)
  local copies, waits for them, and re-layouts: 6.5 us -> 2.25 us
  Pallas kernels: 19.8 us -> 20.8 us
    unnamed x14 -> x4, local copies, waits for them, and re-layouts: 6.5 us -> 2.25 us
    pallas_call x1, Pallas kernels: 19.8 us -> 20.8 us  [shards(): pl.pallas_call(functools.partial(kernel, n_wl, n_tile, n_wave, cols, bloc...]
where the time goes in v1:
time: 23.9 us; the launch traced here: 23.7 us
  Pallas kernels  20.8 us (87%)
  local copies, waits for them, and re-layouts  2.25 us (9%)
  between operations  0.65 us (3%)
    pallas_call x1, Pallas kernels, shards(): pl.pallas_call(functools.partial(kernel, n_wl, n_tile, n_wave, cols, bloc...  20.8 us
    unnamed x4, local copies, waits for them, and re-layouts  2.25 us

profile of v1, /device:TPU:1, one launch (start us, length us, event | category | flops | bytes accessed | tf_op | source)
XLA Modules:
  0.0 23.7 jit_solution(14457806585034322163)
XLA Ops:
  0.6 20.8 %shard_map.77 = (f32[2,8,4096]{2,1,0:T(8,128)}, f32[2,256]{1,0:T(2,128)}) custom-call(f32[2,256]{1,0:T(2,128)} %dens_hbm.1, s32[4,8,4096]{2,1,0:T(8,128)} %index_hbm.1, bf16[4,8,4096]{2,1,0:T(8,128)(2,1)} %weight_hbm.1, f32[2,8,4096]{2,1,0:T(8,128)} %fwd_hbm.1, f32[2,8,4096]{2,1,0:T(8,128)} %adj_hbm.1, f32[2]{0:T(128)} %omega.1), custom_call_target="tpu_custom_call" | custom-call | flops 40000000 | bytes 2000000 | tf_op jit(solution)/shard_map/pallas_call | solution.py:392
  21.4 0.0 copy-start
  21.4 1.7 %copy.10 = f32[2,8,4096]{2,1,0:T(8,128)} copy(f32[2,8,4096]{2,1,0:T(8,128)} %get-tuple-element.4) | data formatting | bytes 524288
  23.1 0.0 copy-done
  23.1 0.6 %copy.11 = f32[2,256]{1,0:T(2,128)} copy(f32[2,256]{1,0:T(2,128)S(1)} %copy-done) | data formatting | bytes 4096
Async XLA Ops:
  21.4 1.7 %copy-start = (f32[2,256]{1,0:T(2,128)S(1)}, f32[2,256]{1,0:T(2,128)}, u32[]{:S(2)}) copy-start(f32[2,256]{1,0:T(2,128)} %get-tuple-element.5) | copy-start | bytes 6148

commit v2 on v1

--- a/solution.py
+++ b/solution.py
@@ -152,9 +152,27 @@
     def spread(w, t):
         return jnp.concatenate([drive[w * ITERS + t]] * CELLS, axis=1)
 
-    loads[2].wait()
     loads[3].wait()
     loads[4].wait()
+    own = lax.broadcasted_iota(jnp.int32, (8, LANES), 1) // CELLS
+
+    def weigh(g, carry):
+        start = pl.multiple_of(g * LANES, LANES)
+        base = own + g * (LANES // CELLS)
+        shifts = [index[f, :, pl.ds(start, LANES)] - base for f in range(index.shape[0])]
+        values = [weight[f, :, pl.ds(start, LANES)].astype(jnp.float32) for f in range(index.shape[0])]
+        for r in range(2):
+            for d in range(OFFSETS):
+                target = r * blocks + d - REACH
+                total = jnp.where(shifts[0] == target, values[0], 0.0)
+                for f in range(1, index.shape[0]):
+                    total = total + jnp.where(shifts[f] == target, values[f], 0.0)
+                matched[r * OFFSETS + d, :, pl.ds(start, LANES)] = total
+        return carry
+
+    lax.fori_loop(0, cols // LANES, weigh, 0, unroll=2)
+
+    loads[2].wait()
     for peer in peers:
         gather_to(wl, peer).wait_recv()
     for i in range(n_wl):
@@ -200,24 +218,6 @@
     send_dens[0] = density[0, 0:2, :]
     send_dens[1] = density[0, 6:8, :]
     sends((2,), lambda copy: copy.start())
-
-    own = lax.broadcasted_iota(jnp.int32, (8, LANES), 1) // CELLS
-
-    def weigh(g, carry):
-        start = pl.multiple_of(g * LANES, LANES)
-        base = own + g * (LANES // CELLS)
-        shifts = [index[f, :, pl.ds(start, LANES)] - base for f in range(index.shape[0])]
-        values = [weight[f, :, pl.ds(start, LANES)].astype(jnp.float32) for f in range(index.shape[0])]
-        for r in range(2):
-            for d in range(OFFSETS):
-                target = r * blocks + d - REACH
-                total = jnp.where(shifts[0] == target, values[0], 0.0)
-                for f in range(1, index.shape[0]):
-                    total = total + jnp.where(shifts[f] == target, values[f], 0.0)
-                matched[r * OFFSETS + d, :, pl.ds(start, LANES)] = total
-        return carry
-
-    lax.fori_loop(0, cols // LANES, weigh, 0)
 
     arrivals((0, 1))
     for w in range(n_wave):

time: 23.9 us -> 23.9 us (level)
  no operation moved by 1% of the time
where the time goes in v2:
time: 23.9 us; the launch traced here: 23.7 us
  Pallas kernels  20.8 us (87%)
  local copies, waits for them, and re-layouts  2.25 us (9%)
  between operations  0.65 us (3%)
    pallas_call x1, Pallas kernels, shards(): pl.pallas_call(functools.partial(kernel, n_wl, n_tile, n_wave, cols, bloc...  20.8 us
    unnamed x4, local copies, waits for them, and re-layouts  2.25 us

profile of v2, /device:TPU:1, one launch (start us, length us, event | category | flops | bytes accessed | tf_op | source)
XLA Modules:
  0.0 23.7 jit_solution(5658280965145992828)
XLA Ops:
  0.6 20.8 %shard_map.77 = (f32[2,8,4096]{2,1,0:T(8,128)}, f32[2,256]{1,0:T(2,128)}) custom-call(f32[2,256]{1,0:T(2,128)} %dens_hbm.1, s32[4,8,4096]{2,1,0:T(8,128)} %index_hbm.1, bf16[4,8,4096]{2,1,0:T(8,128)(2,1)} %weight_hbm.1, f32[2,8,4096]{2,1,0:T(8,128)} %fwd_hbm.1, f32[2,8,4096]{2,1,0:T(8,128)} %adj_hbm.1, f32[2]{0:T(128)} %omega.1), custom_call_target="tpu_custom_call" | custom-call | flops 40000000 | bytes 2000000 | tf_op jit(solution)/shard_map/pallas_call | solution.py:392
  21.4 0.0 copy-start
  21.4 1.7 %copy.10 = f32[2,8,4096]{2,1,0:T(8,128)} copy(f32[2,8,4096]{2,1,0:T(8,128)} %get-tuple-element.4) | data formatting | bytes 524288
  23.1 0.0 copy-done
  23.1 0.6 %copy.11 = f32[2,256]{1,0:T(2,128)} copy(f32[2,256]{1,0:T(2,128)S(1)} %copy-done) | data formatting | bytes 4096
Async XLA Ops:
  21.4 1.7 %copy-start = (f32[2,256]{1,0:T(2,128)S(1)}, f32[2,256]{1,0:T(2,128)}, u32[]{:S(2)}) copy-start(f32[2,256]{1,0:T(2,128)} %get-tuple-element.5) | copy-start | bytes 6148

commit v3 on v2

--- a/solution.py
+++ b/solution.py
@@ -214,7 +214,7 @@
             inverse[0, :, pl.ds(start, LANES)] = time_step / (1.0 + high_contrast * total)
         return carry
 
-    lax.fori_loop(0, chunks, cell_density, 0)
+    lax.fori_loop(0, chunks, cell_density, 0, unroll=2)
     send_dens[0] = density[0, 0:2, :]
     send_dens[1] = density[0, 6:8, :]
     sends((2,), lambda copy: copy.start())
@@ -251,7 +251,7 @@
             rim(w, slabs, slabs[2], where)
         return carry
 
-    lax.fori_loop(0, chunks, start_fields, 0)
+    lax.fori_loop(0, chunks, start_fields, 0, unroll=2)
 
     def mirror(field):
         for w in range(n_wave):
@@ -276,7 +276,7 @@
         inverse[1, :, where] = jnp.where(beyond, 0.0, time_step / (1.0 + high_contrast * density[1, :, where]))
         return carry
 
-    lax.fori_loop(0, chunks, invert, 0)
+    lax.fori_loop(0, chunks, invert, 0, unroll=4)
 
     def advance(t, old, g, w, s):
         where = pl.ds(pl.multiple_of(g * WIDTH, WIDTH), WIDTH)
@@ -314,7 +314,7 @@
                     edge[w, 2, 4 * run + 2 : 4 * run + 3, where] = slabs[run][7:8, :]
             return carry
 
-        lax.fori_loop(0, chunks, step, 0)
+        lax.fori_loop(0, chunks, step, 0, unroll=2)
         mirror(new)
 
     def last(g, carry):
@@ -342,7 +342,7 @@
             pooled[k, :, out] = sums[8 * k : 8 * k + 8, :]
         return carry
 
-    lax.fori_loop(0, chunks, last, 0)
+    lax.fori_loop(0, chunks, last, 0, unroll=2)
     store = pltpu.make_async_copy(final, field_hbm, local_sem.at[5])
     store.start()
 

time: 23.9 us -> 21.9 us (0.916)
  Pallas kernels: 20.8 us -> 18.8 us
    pallas_call x1, Pallas kernels: 20.8 us -> 18.8 us  [shards(): pl.pallas_call(functools.partial(kernel, n_wl, n_tile, n_wave, cols, bloc...]
where the time goes in v3:
time: 21.9 us; the launch traced here: 21.7 us
  Pallas kernels  18.8 us (86%)
  local copies, waits for them, and re-layouts  2.25 us (10%)
  between operations  0.65 us (3%)
    pallas_call x1, Pallas kernels, shards(): pl.pallas_call(functools.partial(kernel, n_wl, n_tile, n_wave, cols, bloc...  18.8 us
    unnamed x4, local copies, waits for them, and re-layouts  2.25 us

profile of v3, /device:TPU:1, one launch (start us, length us, event | category | flops | bytes accessed | tf_op | source)
XLA Modules:
  0.0 21.7 jit_solution(9650161439792439109)
XLA Ops:
  0.6 18.8 %shard_map.77 = (f32[2,8,4096]{2,1,0:T(8,128)}, f32[2,256]{1,0:T(2,128)}) custom-call(f32[2,256]{1,0:T(2,128)} %dens_hbm.1, s32[4,8,4096]{2,1,0:T(8,128)} %index_hbm.1, bf16[4,8,4096]{2,1,0:T(8,128)(2,1)} %weight_hbm.1, f32[2,8,4096]{2,1,0:T(8,128)} %fwd_hbm.1, f32[2,8,4096]{2,1,0:T(8,128)} %adj_hbm.1, f32[2]{0:T(128)} %omega.1), custom_call_target="tpu_custom_call" | custom-call | flops 40000000 | bytes 2000000 | tf_op jit(solution)/shard_map/pallas_call | solution.py:392
  19.4 0.0 copy-start
  19.5 1.7 %copy.10 = f32[2,8,4096]{2,1,0:T(8,128)} copy(f32[2,8,4096]{2,1,0:T(8,128)} %get-tuple-element.4) | data formatting | bytes 524288
  21.1 0.0 copy-done
  21.1 0.6 %copy.11 = f32[2,256]{1,0:T(2,128)} copy(f32[2,256]{1,0:T(2,128)S(1)} %copy-done) | data formatting | bytes 4096
Async XLA Ops:
  19.4 1.7 %copy-start = (f32[2,256]{1,0:T(2,128)S(1)}, f32[2,256]{1,0:T(2,128)}, u32[]{:S(2)}) copy-start(f32[2,256]{1,0:T(2,128)} %get-tuple-element.5) | copy-start | bytes 6148
